TPU v7x, 128 devices: a whole 4x4x4 slice. The times are simulated.
128 devices in a mesh: pipe: 2 (over y_hi), seq: 16 (over x, z), dp: 4 (over y_lo, core).
Axes of the slice: x: 4, y: 4 (y_hi: 2, y_lo: 2; y = y_hi * 2 + y_lo), z: 4, core: 2. Of those that a mesh axis runs over, the one named last changes fastest.
Arguments:
- queries: bfloat16 [2, 4, 16, 384, 1536], P('pipe', 'dp', 'seq'), may hold values from -18 to 18
- keys: bfloat16 [2, 4, 16, 384, 1536], P('pipe', 'dp', 'seq'), may hold values from -18 to 18
- values: bfloat16 [2, 4, 16, 384, 1536], P('pipe', 'dp', 'seq'), may hold values from -6 to 6
- grad_out: bfloat16 [2, 4, 16, 384, 1536], P('pipe', 'dp', 'seq'), may hold values from -20 to 20
- norm_gains: float32 [2, 2, 128], P('pipe'), may hold values from 0.5 to 1.5
- kv_tiles: int32 [2, 4, 16, 3], P('pipe', 'dp', 'seq'), may hold values from -1 to 15, as said below
Outputs:
- qkv_grad: bfloat16 [2, 3, 4, 16, 384, 1536], P('pipe', None, 'dp', 'seq')
- gain_grads: float32 [2, 2, 128], P('pipe')
Inputs may be any that keep to these rules, and one draw needn't show every extreme that they name: `kv_tiles`: tile t covers frame tile t // 1 and spatial tile t % 1. The row of tile t names tile t itself and some of the other tiles of frame tiles t - 1, t // 1 and t + 1 inside the sample, each at most once, in some order; its other entries are -1.
All inputs are finite; a program needn't handle non-finite values.
Results may differ from a plain program's by a relative error of at most 0.007.
Values may be sent and summed in bfloat16 or wider, within the bound.
A program may use at most 256 MiB of HBM per device.

v0:
```python
import math

import jax
import jax.numpy as jnp
from jax import lax
from jax.sharding import PartitionSpec as P

HEADS = 12
HEAD_DIM = 128


epsilon = 1e-06


def padded(shard, sides, width):
    for axis, dim in sides:
        size, length = (lax.axis_size(axis), shard.shape[dim])
        up = [(i, (i + 1) % size) for i in range(size - 1)]
        down = [(j, i) for i, j in up]
        last = lax.slice_in_dim(shard, length - width, length, axis=dim)
        initial = lax.slice_in_dim(shard, 0, width, axis=dim)
        before = lax.ppermute(last, axis, up)
        after = lax.ppermute(initial, axis, down)
        shard = jnp.concatenate([before, shard, after], axis=dim)
    return shard


def passed_along(value, axis, steps):
    count = lax.axis_size(axis)
    initial, last = (max(0, -steps), min(count, count - steps))
    return lax.ppermute(value, axis, [(source, source + steps) for source in range(initial, last)])


def passed_along_2(value, axis, steps):
    count = lax.axis_size(axis)
    pairs = [(source, (source + steps) % count) for source in range(count)]
    return lax.ppermute(value, axis, pairs)


def normalize(source, gain_row):
    floats = source.astype(jnp.float32).reshape(source.shape[:-1] + (HEADS, HEAD_DIM))
    scaled = lax.rsqrt(jnp.mean(floats * floats, axis=-1, keepdims=True) + epsilon)
    normed = (floats * scaled * gain_row).astype(jnp.bfloat16).reshape(source.shape)
    return (normed, floats, scaled)


def norm_back(grad_hat, floats, scaled, gain_row):
    projected = jnp.sum(gain_row * grad_hat * floats, axis=-1, keepdims=True)
    gradient = scaled * gain_row * grad_hat - scaled**3 * floats * projected / HEAD_DIM
    gain_part = jnp.sum((grad_hat * floats * scaled).reshape(-1, HEAD_DIM), axis=0)
    return (gradient.reshape(gradient.shape[:-2] + (HEADS * HEAD_DIM,)), gain_part)


def score_block(query_head, grad_head, key_head, value_head, key_mask):
    root_scale = HEAD_DIM ** (-0.5)
    scores = (
        jnp.einsum("nqhd,nkhd->nhqk", query_head, key_head, preferred_element_type=jnp.float32)
        * root_scale
    )
    exp_scores = jnp.exp(scores) * key_mask[:, None, None, :]
    grad_attn = jnp.einsum(
        "nqhd,nkhd->nhqk", grad_head, value_head, preferred_element_type=jnp.float32
    )
    totals = jnp.sum(exp_scores, axis=-1, keepdims=True)
    attention = exp_scores / totals
    deltas = jnp.sum(attention * grad_attn, axis=-1, keepdims=True)
    dscore = (attention * (grad_attn - deltas)).astype(jnp.bfloat16)
    return (dscore, attention.astype(jnp.bfloat16), totals, deltas)


def spread(slot_grad, targets, list_slots, target_span):
    row_count, key_rows, head_count, head_width = slot_grad.shape
    shaped = slot_grad.reshape(
        row_count * list_slots, key_rows // list_slots, head_count * head_width
    )
    flat_targets = targets.reshape(-1)
    placed = jnp.where(flat_targets >= 0, flat_targets, target_span)
    totals = jnp.zeros(
        (target_span + 1, key_rows // list_slots, head_count * head_width), jnp.float32
    )
    return totals.at[placed].add(shaped)[:target_span]


def tile_pass(
    query_hat, grad_in, key_gathered, value_gathered, key_mask, targets, list_slots, target_span
):
    row_count, tile_rows, lane_total = query_hat.shape
    key_rows = key_gathered.shape[1]
    root_scale = HEAD_DIM ** (-0.5)
    query_parts, key_parts, value_parts, total_parts, delta_parts = ([], [], [], [], [])
    for first_head in range(0, HEADS, 2):
        lane_span = slice(first_head * HEAD_DIM, (first_head + 2) * HEAD_DIM)
        query_head = query_hat[:, :, lane_span].reshape(row_count, tile_rows, 2, HEAD_DIM)
        grad_head = grad_in[:, :, lane_span].reshape(row_count, tile_rows, 2, HEAD_DIM)
        key_head = key_gathered[:, :, lane_span].reshape(row_count, key_rows, 2, HEAD_DIM)
        value_head = value_gathered[:, :, lane_span].reshape(row_count, key_rows, 2, HEAD_DIM)
        dscore, attn_low, totals, deltas = score_block(
            query_head, grad_head, key_head, value_head, key_mask
        )
        query_parts.append(
            jnp.einsum("nhqk,nkhd->nqhd", dscore, key_head, preferred_element_type=jnp.float32)
            * root_scale
        )
        key_slot = (
            jnp.einsum("nhqk,nqhd->nkhd", dscore, query_head, preferred_element_type=jnp.float32)
            * root_scale
        )
        value_slot = jnp.einsum(
            "nhqk,nqhd->nkhd", attn_low, grad_head, preferred_element_type=jnp.float32
        )
        key_parts.append(spread(key_slot, targets, list_slots, target_span))
        value_parts.append(spread(value_slot, targets, list_slots, target_span))
        total_parts.append(totals[..., 0])
        delta_parts.append(deltas[..., 0])
    query_grads = jnp.concatenate(query_parts, axis=2)
    return (
        query_grads,
        jnp.concatenate(key_parts, axis=-1),
        jnp.concatenate(value_parts, axis=-1),
        jnp.concatenate(total_parts, axis=1),
        jnp.concatenate(delta_parts, axis=1),
    )


def local(queries, keys, values, grad_out, norm_gains, kv_tiles):
    query_in = queries[0, 0]
    key_in = keys[0, 0]
    value_in = values[0, 0]
    grad_in = grad_out[0, 0]
    gain_rows = norm_gains[0]
    tile_lists = kv_tiles[0, 0]
    tiles_here, tile_rows, lane_total = query_in.shape
    list_slots = tile_lists.shape[1]
    position = lax.axis_index("seq")
    seq_count = lax.axis_size("seq")
    query_hat, query_floats, query_scale = normalize(query_in, gain_rows[0])
    key_hat, key_floats, key_scale = normalize(key_in, gain_rows[1])
    rim_pairs = padded(jnp.stack([key_hat, value_in]), (("seq", 1),), tiles_here)
    live_slots = tile_lists >= 0
    key_mask = jnp.repeat(live_slots.astype(jnp.float32), tile_rows, axis=1)
    local_ids = tile_lists - (position - 1) * tiles_here
    fetch_ids = jnp.clip(local_ids, 0, 3 * tiles_here - 1)
    key_gathered = rim_pairs[0][fetch_ids].reshape(tiles_here, list_slots * tile_rows, lane_total)
    value_gathered = rim_pairs[1][fetch_ids].reshape(tiles_here, list_slots * tile_rows, lane_total)
    targets = jnp.where(live_slots, local_ids, -1)
    target_span = 3 * tiles_here
    query_hat_grad, key_acc, value_acc, totals, deltas = tile_pass(
        query_hat, grad_in, key_gathered, value_gathered, key_mask, targets, list_slots, target_span
    )
    query_grad, query_gain = norm_back(query_hat_grad, query_floats, query_scale, gain_rows[0])
    query_low = query_grad.astype(jnp.bfloat16)
    from_right = passed_along(jnp.stack([key_acc[:tiles_here], value_acc[:tiles_here]]), "seq", -1)
    from_left = passed_along(
        jnp.stack([key_acc[2 * tiles_here :], value_acc[2 * tiles_here :]]), "seq", 1
    )
    key_hat_grad = key_acc[tiles_here : 2 * tiles_here] + from_right[0] + from_left[0]
    value_grad = value_acc[tiles_here : 2 * tiles_here] + from_right[1] + from_left[1]
    key_grad, key_gain = norm_back(
        key_hat_grad.reshape(tiles_here, tile_rows, HEADS, HEAD_DIM),
        key_floats,
        key_scale,
        gain_rows[1],
    )
    summed = lax.psum(jnp.stack([query_gain, key_gain]), ("seq", "dp"))
    gain_grads = summed / math.sqrt(
        lax.axis_size("dp") * seq_count * tiles_here * tile_rows * HEADS
    )
    key_low = key_grad.astype(jnp.bfloat16)
    value_low = value_grad.astype(jnp.bfloat16)
    passed = passed_along_2(jnp.stack([query_low, key_low, value_low]), "pipe", -1)
    return (passed[None, :, None], gain_grads[None])


def solution(mesh):
    placed = (
        P("pipe", "dp", "seq", None, None),
        P("pipe", "dp", "seq", None, None),
        P("pipe", "dp", "seq", None, None),
        P("pipe", "dp", "seq", None, None),
        P("pipe", None, None),
        P("pipe", "dp", "seq", None),
    )
    return jax.shard_map(
        local,
        mesh=mesh,
        in_specs=placed,
        out_specs=(P("pipe", None, "dp", "seq", None, None), P("pipe", None, None)),
        check_vma=False,
    )
```

profile of v0, /device:TPU:0, one launch (start us, length us, event | category | flops | bytes accessed | tf_op | source)
XLA Modules:
  0.0 747.5 jit_solution(4585193369530839053)
XLA Ops:
  10.4 5.4 collective-permute-start
  40.5 24.8 %collective-permute-done = bf16[2,1,384,1536]{3,2,1,0:T(8,128)(2,1)} collective-permute-done((bf16[2,1,384,1536]{3,2,1,0:T(8,128)(2,1)}, bf16[2,1,384,1536]{3,2,1,0:T(8,128)(2,1)}, u32[]{:S(2)}, u32[]{:S(2)}) %collective-permute-start) | collective-permute-done | bytes 2359328 | tf_op jit(solution)/shard_map/ppermute | solution.py:22
  65.3 5.5 collective-permute-done.1
  74.3 3.8 slice_bitcast_fusion
  78.1 4.7 gather_fusion.1
  87.3 4.7 gather_fusion
  92.0 3.6 fusion.84
  97.8 3.6 convolution_bitcast_fusion.5
  101.3 5.2 multiply_reduce_fusion.5
  106.6 4.0 convolution_bitcast_fusion.11
  110.5 3.6 multiply_convert_fusion.5
  118.4 3.6 convolution_bitcast_fusion.4
  122.0 5.2 multiply_reduce_fusion.4
  127.2 4.0 convolution_bitcast_fusion.10
  131.2 3.7 multiply_convert_fusion.4
  139.2 3.6 convolution_bitcast_fusion.3
  142.7 5.2 multiply_reduce_fusion.3
  148.0 4.0 convolution_bitcast_fusion.9
  151.9 3.8 multiply_convert_fusion.3
  160.0 3.6 convolution_bitcast_fusion.2
  163.6 5.2 multiply_reduce_fusion.2
  168.8 4.0 convolution_bitcast_fusion.8
  172.8 3.7 multiply_convert_fusion.2
  180.8 3.6 convolution_bitcast_fusion.1
  184.3 5.2 multiply_reduce_fusion.1
  189.6 4.0 convolution_bitcast_fusion.7
  193.6 3.7 multiply_convert_fusion.1
  198.6 3.8 convolution_bitcast_fusion
  202.4 5.0 multiply_reduce_fusion
  207.4 4.0 convolution_bitcast_fusion.6
  211.4 3.7 multiply_convert_fusion
  297.3 5.0 slice_bitcast_fusion.9
  302.3 4.3 copy.292
  308.6 4.7 copy.289
  323.0 4.3 copy.295
  329.2 4.9 copy.298
  336.1 4.7 copy.301
  342.9 4.7 copy.304
  380.3 3.8 scatter_fusion.11
  395.9 6.7 collective-permute-start.3
  422.2 74.4 %collective-permute-done.2 = f32[2,1,384,1536]{3,2,1,0:T(8,128)} collective-permute-done((f32[2,1,384,1536]{3,2,1,0:T(8,128)}, f32[2,1,384,1536]{3,2,1,0:T(8,128)}, u32[]{:S(2)}, u32[]{:S(2)}) %collective-permute-start.2) | collective-permute-done | bytes 4718624 | tf_op jit(solution)/shard_map/ppermute | solution.py:31
  496.6 3.7 collective-permute-done.3
  500.3 7.3 fusion.21
  509.5 4.9 multiply_reduce_fusion.8
  523.9 4.5 fusion.65
  552.2 3.6 multiply_reduce_fusion.6
  555.8 186.9 %psum.7 = f32[2,128]{1,0:T(2,128)S(1)} all-reduce(f32[2,128]{1,0:T(2,128)S(1)} %pad_maximum_fusion.5), channel_id=1, replica_groups=mesh['pipe'=2,'seq'=16,'dp'=4] {'seq','dp'}, use_global_device_ids=true, to_apply=%region_31.32 | all-reduce | flops 256 | bytes 2048 | tf_op jit(solution)/shard_map/psum | solution.py:164
  743.3 4.0 copy.394
  (289 shorter events, 262.2 us)
Async XLA Ops:
  7.0 15.9 %copy-start.70 = (f32[128]{0:T(128)}, f32[128]{0:T(128)S(1)}, u32[]{:S(2)}) copy-start(f32[128]{0:T(128)S(1)} %get-tuple-element.45) | copy-start | bytes 1540
  8.8 8.3 %copy-start.55 = (bf16[1,1,1,384,1536]{4,3,2,1,0:T(8,128)(2,1)S(1)}, bf16[1,1,1,384,1536]{4,3,2,1,0:T(8,128)(2,1)}, u32[]{:S(2)}) copy-start(bf16[1,1,1,384,1536]{4,3,2,1,0:T(8,128)(2,1)} %param.9) | copy-start | bytes 3538948
  10.4 8.2 %copy-start.7 = (bf16[1,1,1,384,1536]{4,3,2,1,0:T(8,128)(2,1)S(1)}, bf16[1,1,1,384,1536]{4,3,2,1,0:T(8,128)(2,1)}, u32[]{:S(2)}) copy-start(bf16[1,1,1,384,1536]{4,3,2,1,0:T(8,128)(2,1)} %param.6) | copy-start | bytes 3538948
  10.4 54.8 %collective-permute-start = (bf16[2,1,384,1536]{3,2,1,0:T(8,128)(2,1)}, bf16[2,1,384,1536]{3,2,1,0:T(8,128)(2,1)}, u32[]{:S(2)}, u32[]{:S(2)}) collective-permute-start(bf16[2,1,384,1536]{3,2,1,0:T(8,128)(2,1)} %pad_maximum_fusion.4), channel_id=1, source_target_pairs={{0,4},{4,8},{8,12},{12,16},{16,20},{20,24},{24,28},{28,32},{32,36}... | collective-permute-start | bytes 7077896 | tf_op jit(solution)/shard_map/ppermute | solution.py:22
  15.9 54.9 %collective-permute-start.1 = (bf16[2,1,384,1536]{3,2,1,0:T(8,128)(2,1)}, bf16[2,1,384,1536]{3,2,1,0:T(8,128)(2,1)}, u32[]{:S(2)}, u32[]{:S(2)}) collective-permute-start(bf16[2,1,384,1536]{3,2,1,0:T(8,128)(2,1)} %pad_maximum_fusion.4), channel_id=1, source_target_pairs={{4,0},{8,4},{12,8},{16,12},{20,16},{24,20},{28,24},{32,28},{36,32}... | collective-permute-start | bytes 7077896 | tf_op jit(solution)/shard_map/ppermute | solution.py:23
  20.8 381.8 %copy-start = (f32[384,12,128]{0,2,1:T(8,128)}, f32[384,12,128]{0,2,1:T(8,128)S(1)}, u32[]{:S(2)}) copy-start(f32[384,12,128]{0,2,1:T(8,128)S(1)} %mul.607) | copy-start | bytes 7077892
  26.0 44.7 %copy-start.24 = (bf16[1,1,384,1536]{3,2,1,0:T(8,128)(2,1)S(1)}, bf16[1,1,384,1536]{3,2,1,0:T(8,128)(2,1)}, u32[]{:S(2)}) copy-start(bf16[1,1,384,1536]{3,2,1,0:T(8,128)(2,1)} %copy-done.23) | copy-start | bytes 3538948
  36.7 34.1 %copy-start.33 = (bf16[1,1,1,384,1536]{4,3,2,1,0:T(8,128)(2,1)S(1)}, bf16[1,1,1,384,1536]{4,3,2,1,0:T(8,128)(2,1)}, u32[]{:S(2)}) copy-start(bf16[1,1,1,384,1536]{4,3,2,1,0:T(8,128)(2,1)} %param.8) | copy-start | bytes 3538948
  106.6 4.0 copy-start.18
  127.2 4.0 copy-start.19
  148.0 4.0 copy-start.20
  168.8 4.0 copy-start.21
  189.6 4.0 copy-start.22
  198.6 8.9 %copy-start.52 = (bf16[1,1152,256]{1,2,0:T(8,128)(2,1)}, bf16[1,1152,256]{1,2,0:T(8,128)(2,1)S(1)}, u32[]{:S(2)}) copy-start(bf16[1,1152,256]{1,2,0:T(8,128)(2,1)S(1)} %copy.364) | copy-start | bytes 1769476
  198.6 3.8 copy-start.56
  202.4 5.0 copy-start.54
  207.4 4.0 copy-start.17
  211.4 3.7 copy-start.10
  211.4 3.7 copy-start.58
  258.3 4.5 copy-start.36
  266.1 3.9 copy-start.42
  273.3 3.8 copy-start.40
  280.4 3.8 copy-start.39
  287.6 3.8 copy-start.38
  297.3 5.0 copy-start.34
  354.7 3.8 copy-start.45
  362.0 3.9 copy-start.44
  369.2 3.8 copy-start.43
  376.4 3.9 copy-start.37
  386.5 3.1 copy-start.30
  389.6 3.9 copy-start.29
  392.1 104.5 %collective-permute-start.2 = (f32[2,1,384,1536]{3,2,1,0:T(8,128)}, f32[2,1,384,1536]{3,2,1,0:T(8,128)}, u32[]{:S(2)}, u32[]{:S(2)}) collective-permute-start(f32[2,1,384,1536]{3,2,1,0:T(8,128)} %pad_maximum_fusion.1), channel_id=1, source_target_pairs={{4,0},{8,4},{12,8},{16,12},{20,16},{24,20},{28,24},{32,28},{36,32}... | collective-permute-start | bytes 14155784 | tf_op jit(solution)/shard_map/ppermute | solution.py:31
  395.9 104.3 %collective-permute-start.3 = (f32[2,1,384,1536]{3,2,1,0:T(8,128)}, f32[2,1,384,1536]{3,2,1,0:T(8,128)}, u32[]{:S(2)}, u32[]{:S(2)}) collective-permute-start(f32[2,1,384,1536]{3,2,1,0:T(8,128)} %pad_maximum_fusion.2), channel_id=1, source_target_pairs={{0,4},{4,8},{8,12},{12,16},{16,20},{20,24},{24,28},{28,32},{32,36}... | collective-permute-start | bytes 14155784 | tf_op jit(solution)/shard_map/ppermute | solution.py:31
  406.2 3.3 copy-start.4
  411.6 4.3 copy-start.48
  413.6 3.0 copy-start.13
  413.6 3.0 copy-start.49
  520.7 3.2 copy-start.6
  520.7 3.2 copy-start.65
  523.9 4.6 copy-start.8
  523.9 4.6 copy-start.25
  523.9 4.8 copy-start.26
  523.9 5.5 copy-start.27
  523.9 6.2 copy-start.28
  523.9 6.2 copy-start.67
  533.3 210.0 %collective-permute-start.4 = (bf16[3,1,384,1536]{3,2,1,0:T(8,128)(2,1)}, bf16[3,1,384,1536]{3,2,1,0:T(8,128)(2,1)}, u32[]{:S(2)}, u32[]{:S(2)}) collective-permute-start(bf16[3,1,384,1536]{3,2,1,0:T(8,128)(2,1)} %pad_maximum_fusion.3), channel_id=1, source_target_pairs={{0,64},{64,0},{1,65},{65,1},{2,66},{66,2},{3,67},{67,3},{4,68},{68... | collective-permute-start | bytes 10616840 | tf_op jit(solution)/shard_map/ppermute | solution.py:37
  540.7 3.1 copy-start.59
  544.6 3.2 copy-start.9
  (31 other events, 58.5 us)
where the time goes:
time: 755 us; the launch traced here: 747 us
  local copies, waits for them, and re-layouts  235 us (31%)
  blocking collectives  187 us (25%)
  waiting for transfers between devices  108 us (14%)
  other arithmetic  106 us (14%)
  matrix products  91.6 us (12%)
  starting transfers between devices  18 us (2%)
    psum x1, blocking collectives, local(): summed = lax.psum(jnp.stack([query_gain, key_gain]), ('seq', 'dp'))  187 us
    ppermute x2, waiting for transfers between devices, passed_along(): lax.ppermute(value, axis, [(source, source + steps) for source in range(i...  78.1 us
    unnamed x172, local copies, waits for them, and re-layouts  58.3 us
    scatter-add x12, other arithmetic, spread(): return totals.at[placed].add(shaped)[:target_span]  41 us
    div x6, matrix products, score_block(): attention = exp_scores / totals  31.2 us
    reshape x12, local copies, waits for them, and re-layouts, spread(): slot_grad.reshape(row_count * list_slots, key_rows // list_slots, head_co...  30 us
    transpose x6, local copies, waits for them, and re-layouts, tile_pass(): jnp.einsum('nhqk,nqhd->nkhd', attn_low, grad_head, preferred_element_type...  27.7 us
    ppermute x1, waiting for transfers between devices, padded(): before = lax.ppermute(last, axis, up)  24.8 us
  transfers between devices with their start and end apart: 5, of which 4 were waited for; matrix products, arithmetic and copies ran while one was open for 9% of the time, Pallas kernels for 0%

commit v1 on v0

v1 whole, which is shorter than its diff:
```python
import math

import jax
import jax.numpy as jnp
from jax import lax
from jax.experimental import pallas as pl
from jax.experimental.pallas import tpu as pltpu
from jax.sharding import PartitionSpec as P

HEADS = 12
DIM = 128
TILE = 384
SPAN = 3 * TILE
EPSILON = 1e-06
SCALE = DIM**-0.5
EXP2_SCALE = SCALE * math.log2(math.e)
MESH = pl.DeviceIdType.MESH
BF16, F32 = jnp.bfloat16, jnp.float32

TOTAL_LAG, GRAD_LAG, QUERY_LAG, AHEAD = 1, 2, 4, 2
SLOTS = GRAD_LAG + 1
STEPS = HEADS + QUERY_LAG


def over_rows(a, b):
    return lax.dot_general(a, b, (((1,), (1,)), ((), ())), preferred_element_type=F32)


def product(a, b):
    return lax.dot_general(a, b, (((1,), (0,)), ((), ())), preferred_element_type=F32)


def inverse_norm(x):
    return lax.rsqrt(jnp.mean(x * x, axis=-1, keepdims=True) + EPSILON)


def norm_back(grad_hat, x, gain):
    inverse = inverse_norm(x)
    scaled = grad_hat * x
    projected = jnp.sum(gain * scaled, axis=-1, keepdims=True)
    grad = inverse * (gain * grad_hat) - x * (inverse * inverse * inverse * projected * (1.0 / DIM))
    return grad, jnp.sum(scaled * inverse, axis=0, keepdims=True)


def kernel(
    seqs, dps, zs,
    q_ref, k_ref, v_ref, g_ref, gain_ref, list_ref,
    out_ref, gain_out,
    q_raw, k_raw, v_in, pair, k_hat, k_turned, exps, gprobs, low, stat_own, stat_out, stat_in,
    tot_own, tot_out, tot_in, dq_own, dq_out, dq_in, results, gain_acc, gain_slots,
    load_sem, in_send, in_recv, stat_send, stat_recv, tot_send, tot_recv, dq_send, dq_recv,
    out_send, out_recv, gain_send, gain_recv,
):
    p, s, d = lax.axis_index("pipe"), lax.axis_index("seq"), lax.axis_index("dp")
    left, right = (p, lax.rem(s + seqs - 1, seqs), d), (p, lax.rem(s + 1, seqs), d)
    sides = (left, right)
    across = (1 - p, s, d)
    xs = seqs // zs
    x, z = s // zs, lax.rem(s, zs)
    groups = (
        (d, dps, lambda i: (p, s, i)),
        (x, xs, lambda i: (p, i * zs + z, d)),
        (z, zs, lambda i: (p, x * zs + i, d)),
    )

    def load(part, source, target, h):
        columns = pl.ds(pl.multiple_of(h * DIM, DIM), DIM)
        return pltpu.make_async_copy(source.at[:, columns], target, load_sem.at[part, h])

    def loads(h):
        return (
            load(0, q_ref, q_raw.at[h], h),
            load(1, k_ref, k_raw.at[h], h),
            load(2, g_ref, pair.at[h, 1, pl.ds(TILE, TILE)], h),
            load(3, v_ref, v_in.at[h], h),
        )

    def start_loads(h, carry):
        for copy in loads(h):
            copy.start()
        return carry

    lax.fori_loop(0, HEADS, start_loads, 0)

    barrier = pltpu.get_barrier_semaphore()
    greeted = [left, right, across]
    for mine, size, device in groups:
        greeted += [device(lax.rem(mine + j, size)) for j in range(1, size)]
    for device in greeted:
        pl.semaphore_signal(barrier, inc=1, device_id=device, device_id_type=MESH)

    def remote(source, target, send, recv, device):
        return pltpu.make_async_remote_copy(
            src_ref=source, dst_ref=target, send_sem=send, recv_sem=recv,
            device_id=device, device_id_type=MESH,
        )

    def send_pair(h, side):
        return remote(
            pair.at[h, :, pl.ds(TILE, TILE)], pair.at[h, :, pl.ds(2 * TILE * (1 - side), TILE)],
            in_send.at[h, side], in_recv.at[h, 1 - side], sides[side],
        )

    def send_block(out, into, send, recv):
        def copy(h, side):
            return remote(
                out.at[h, side], into.at[h, 1 - side], send.at[h, side], recv.at[h, 1 - side], sides[side]
            )
        return copy

    def take(copy, h):
        for side in (0, 1):
            copy(h, side).wait_recv()

    send_stat = send_block(stat_out, stat_in, stat_send, stat_recv)
    send_total = send_block(tot_out, tot_in, tot_send, tot_recv)
    send_dq = send_block(dq_out, dq_in, dq_send, dq_recv)

    def send_result(part, h):
        columns = pl.ds(pl.multiple_of(h * DIM, DIM), DIM)
        return remote(
            results.at[part, h], out_ref.at[part, :, columns],
            out_send.at[part, h], out_recv.at[part, h], across,
        )

    gains = [gain_ref[i : i + 1, :] for i in (0, 1)]

    def names(tile):
        named = (list_ref[0, 0] == tile) | (list_ref[0, 1] == tile) | (list_ref[0, 2] == tile)
        return jnp.where(named, 1.0, 0.0).astype(F32)

    masks = (jnp.where(s > 0, names(s - 1), 0.0), names(s + 1))

    def normalize(h):
        for copy in loads(h):
            copy.wait()
        q = q_raw[h].astype(F32)
        pair[h, 0, TILE : 2 * TILE] = (q * inverse_norm(q) * gains[0]).astype(BF16)

    def normalize_key(h):
        k = k_raw[h].astype(F32)
        hat = k * inverse_norm(k) * gains[1]
        k_hat[h] = hat.astype(BF16)
        k_turned[h] = hat.T.astype(BF16)

    def give_pair(h):
        for side in (0, 1):
            send_pair(h, side).start()

    def scores(h):
        slot = lax.rem(h, SLOTS)
        for b in range(3):
            span = slice(b * TILE, (b + 1) * TILE)
            e = jnp.exp2(over_rows(k_hat[h], pair[h, 0, span]) * EXP2_SCALE)
            g = over_rows(v_in[h], pair[h, 1, span])
            exps[slot, :, span] = e
            gprobs[slot, :, span] = g
            total = jnp.sum(e, axis=0, keepdims=True)
            delta = jnp.sum(e * g, axis=0, keepdims=True)
            target = stat_own.at[h] if b == 1 else stat_out.at[h, b // 2]
            target[0:1] = total
            target[1:2] = delta
        for side in (0, 1):
            send_stat(h, side).start()

    def totals(h):
        take(send_stat, h)
        both = stat_own[h] + masks[0] * stat_in[h, 0] + masks[1] * stat_in[h, 1]
        inverse = 1.0 / both[0:1]
        delta = both[1:2] * inverse
        tot_own[h, 0:1] = inverse
        tot_own[h, 1:2] = delta
        for side in (0, 1):
            tot_out[h, side, 0:1] = inverse * masks[side]
            tot_out[h, side, 1:2] = delta
            send_total(h, side).start()

    def grads(h):
        take(send_total, h)
        slot = lax.rem(h, SLOTS)
        for b in range(3):
            span = slice(b * TILE, (b + 1) * TILE)
            row = tot_own.at[h] if b == 1 else tot_in.at[h, b // 2]
            probs = exps[slot, :, span] * row[0:1]
            low[0, :, span] = probs.astype(BF16)
            low[1, :, span] = (probs * (gprobs[slot, :, span] - row[1:2])).astype(BF16)
        turned = product(k_turned[h], low[1])
        dq_out[h, 0] = turned[:, :TILE].astype(BF16)
        dq_out[h, 1] = turned[:, 2 * TILE :].astype(BF16)
        dq_own[h] = turned[:, TILE : 2 * TILE]
        for side in (0, 1):
            send_dq(h, side).start()
        results[2, h] = product(low[0], pair[h, 1]).astype(BF16)
        send_result(2, h).start()
        key_hat_grad = product(low[1], pair[h, 0]) * SCALE
        grad, gain = norm_back(key_hat_grad, k_raw[h].astype(F32), gains[1])
        gain_acc[1:2] += gain
        results[1, h] = grad.astype(BF16)
        send_result(1, h).start()

    def query_grads(h):
        take(send_dq, h)
        total = dq_own[h] + dq_in[h, 0].astype(F32) + dq_in[h, 1].astype(F32)
        grad, gain = norm_back((total * SCALE).T, q_raw[h].astype(F32), gains[0])
        gain_acc[0:1] += gain
        results[0, h] = grad.astype(BF16)
        send_result(0, h).start()

    gain_acc[...] = jnp.zeros_like(gain_acc)
    normalize(0)
    pl.semaphore_wait(barrier, len(greeted))
    give_pair(0)
    for h in range(1, AHEAD):
        normalize(h)
        give_pair(h)
    for h in range(AHEAD):
        normalize_key(h)

    def within(i):
        return (i >= 0) & (i < HEADS)

    def step(i, carry):
        @pl.when(within(i - TOTAL_LAG))
        def _():
            totals(i - TOTAL_LAG)

        @pl.when(within(i))
        def _():
            take(send_pair, i)
            scores(i)

        @pl.when(within(i + AHEAD))
        def _():
            normalize(i + AHEAD)
            give_pair(i + AHEAD)
            normalize_key(i + AHEAD)

        @pl.when(within(i - GRAD_LAG))
        def _():
            grads(i - GRAD_LAG)

        @pl.when(within(i - QUERY_LAG))
        def _():
            query_grads(i - QUERY_LAG)

        return carry

    lax.fori_loop(0, STEPS, step, 0)

    for axis, (mine, size, device) in enumerate(groups):
        gain_slots[axis, mine] = gain_acc[...]
        copies = [
            remote(
                gain_slots.at[axis, mine], gain_slots.at[axis, mine],
                gain_send.at[axis, j - 1], gain_recv.at[axis, j - 1], device(lax.rem(mine + j, size)),
            )
            for j in range(1, size)
        ]
        for copy in copies:
            copy.start()
        for j in range(1, size):
            sender = lax.rem(mine + size - j, size)
            remote(
                gain_slots.at[axis, mine], gain_slots.at[axis, sender],
                gain_send.at[axis, j - 1], gain_recv.at[axis, j - 1], device(lax.rem(mine + j, size)),
            ).wait_recv()
        for copy in copies:
            copy.wait_send()
        total = gain_slots[axis, 0]
        for j in range(1, size):
            total = total + gain_slots[axis, j]
        gain_acc[...] = total
    gain_out[...] = gain_acc[...] * (1.0 / math.sqrt(dps * seqs * TILE * HEADS))

    def finish(h, carry):
        for copy in (send_pair, send_stat, send_total, send_dq):
            for side in (0, 1):
                copy(h, side).wait_send()
        for part in range(3):
            send_result(part, h).wait()
        return carry

    lax.fori_loop(0, HEADS, finish, 0)


def solution(mesh):
    seqs, dps = mesh.shape["seq"], mesh.shape["dp"]
    zs = 4
    dma, vmem = pltpu.SemaphoreType.DMA, pltpu.VMEM

    def body(*refs):
        kernel(seqs, dps, zs, *refs)

    call = pl.pallas_call(
        body,
        out_shape=(
            jax.ShapeDtypeStruct((3, TILE, HEADS * DIM), BF16),
            jax.ShapeDtypeStruct((2, DIM), F32),
        ),
        in_specs=[pl.BlockSpec(memory_space=pl.ANY)] * 4
        + [pl.BlockSpec(memory_space=pltpu.VMEM), pl.BlockSpec(memory_space=pltpu.SMEM)],
        out_specs=(pl.BlockSpec(memory_space=pl.ANY), pl.BlockSpec(memory_space=pltpu.VMEM)),
        scratch_shapes=[
            vmem((HEADS, TILE, DIM), BF16),
            vmem((HEADS, TILE, DIM), BF16),
            vmem((HEADS, TILE, DIM), BF16),
            vmem((HEADS, 2, SPAN, DIM), BF16),
            vmem((HEADS, TILE, DIM), BF16),
            vmem((HEADS, DIM, TILE), BF16),
            vmem((SLOTS, TILE, SPAN), F32),
            vmem((SLOTS, TILE, SPAN), F32),
            vmem((2, TILE, SPAN), BF16),
            vmem((HEADS, 2, TILE), F32),
            vmem((HEADS, 2, 2, TILE), F32),
            vmem((HEADS, 2, 2, TILE), F32),
            vmem((HEADS, 2, TILE), F32),
            vmem((HEADS, 2, 2, TILE), F32),
            vmem((HEADS, 2, 2, TILE), F32),
            vmem((HEADS, DIM, TILE), F32),
            vmem((HEADS, 2, DIM, TILE), BF16),
            vmem((HEADS, 2, DIM, TILE), BF16),
            vmem((3, HEADS, TILE, DIM), BF16),
            vmem((2, DIM), F32),
            vmem((3, 4, 2, DIM), F32),
            dma((4, HEADS)),
        ]
        + [dma((HEADS, 2))] * 8
        + [dma((3, HEADS)), dma((3, HEADS)), dma((3, 3)), dma((3, 3))],
        compiler_params=pltpu.CompilerParams(
            collective_id=0, has_side_effects=True, vmem_limit_bytes=58 * 2**20
        ),
        cost_estimate=pl.CostEstimate(
            flops=10 * TILE * SPAN * HEADS * DIM,
            bytes_accessed=7 * 2 * TILE * HEADS * DIM,
            transcendentals=TILE * SPAN * HEADS,
        ),
    )

    def local(queries, keys, values, grad_out, norm_gains, kv_tiles):
        grads, gain_grads = call(
            queries[0, 0, 0], keys[0, 0, 0], values[0, 0, 0], grad_out[0, 0, 0],
            norm_gains[0], kv_tiles[0, 0],
        )
        return grads[None, :, None, None], gain_grads[None]

    tokens = P("pipe", "dp", "seq", None, None)
    return jax.shard_map(
        local,
        mesh=mesh,
        in_specs=(tokens,) * 4 + (P("pipe", None, None), P("pipe", "dp", "seq", None)),
        out_specs=(P("pipe", None, "dp", "seq", None, None), P("pipe", None, None)),
        check_vma=False,
    )
```

time: 755 us -> 123 us (0.16)
  local copies, waits for them, and re-layouts: 235 us -> 4.59 us
  blocking collectives: 187 us -> 0 us
  Pallas kernels: 0 us -> 117 us
  waiting for transfers between devices: 108 us -> 0 us
  other arithmetic: 106 us -> 0 us
  matrix products: 91.6 us -> 0 us
  starting transfers between devices: 18 us -> 0 us
    psum x1 -> x0, blocking collectives: 187 us -> none  [local(): summed = lax.psum(jnp.stack([query_gain, key_gain]), ('seq', 'dp'))]
    pallas_call x0 -> x1, Pallas kernels: none -> 117 us  [local(): call(queries[0, 0, 0], keys[0, 0, 0], values[0, 0, 0], grad_out[0, 0, 0],...]
    ppermute x5 -> x0, waiting for transfers between devices: 108 us -> none  [the longest x2 78.1 us: passed_along(): lax.ppermute(value, axis, [(source, source + steps) for source in range(i...]
    dot_general x24 -> x0, matrix products: 60.3 us -> none  [the longest x6 23.8 us: tile_pass(): jnp.einsum('nhqk,nqhd->nkhd', attn_low, grad_head, preferred_element_type...]
    unnamed x172 -> x4, local copies, waits for them, and re-layouts: 58.3 us -> 4.59 us
    mul x24 -> x0, local copies, waits for them, and re-layouts: 41 us -> none  [the longest x8 16.4 us: norm_back(): scaled ** 3 * floats * projected / HEAD_DIM]
    scatter-add x12 -> x0, other arithmetic: 41 us -> none  [spread(): return totals.at[placed].add(shaped)[:target_span]]
    reshape x13 -> x0, local copies, waits for them, and re-layouts: 31.5 us -> none  [the longest x12 30 us: spread(): slot_grad.reshape(row_count * list_slots, key_rows // list_slots, head_co...]
  transfers between devices with their start and end apart: 5 -> 0, of which waited for: 4 -> 0; matrix products, arithmetic and copies ran while one was open for 9% -> 0% of each run, Pallas kernels for 0% -> 0%
where the time goes in v1:
time: 123 us; the launch traced here: 122 us
  Pallas kernels  117 us (95%)
  local copies, waits for them, and re-layouts  4.59 us (4%)
    pallas_call x1, Pallas kernels, local(): call(queries[0, 0, 0], keys[0, 0, 0], values[0, 0, 0], grad_out[0, 0, 0],...  117 us
    unnamed x4, local copies, waits for them, and re-layouts  4.59 us

profile of v1, /device:TPU:0, one launch (start us, length us, event | category | flops | bytes accessed | tf_op | source)
XLA Modules:
  0.0 122.5 jit_solution(2655522075175593922)
XLA Ops:
  0.6 117.2 %shard_map.77 = (bf16[3,384,1536]{2,1,0:T(8,128)(2,1)}, f32[2,128]{1,0:T(2,128)}) custom-call(bf16[384,1536]{1,0:T(8,128)(2,1)} %bitcast.12, bf16[384,1536]{1,0:T(8,128)(2,1)} %bitcast.13, bf16[384,1536]{1,0:T(8,128)(2,1)} %bitcast.14, bf16[384,1536]{1,0:T(8,128)(2,1)} %bitcast.15, f32[2,128]{1,0:T(2,128)} %bitcast.16, s32[1,3]{1,0:T(1,128)} %bitcast.17), custom_call_target="tpu_custom_call" | custom-call | flops 6794772480 | bytes 8257536 | tf_op jit(solution)/shard_map/pallas_call | solution.py:340
  117.9 0.0 copy-start
  117.9 4.0 %copy.11 = bf16[1,3,1,1,384,1536]{5,4,3,2,1,0:T(8,128)(2,1)} copy(bf16[1,3,1,1,384,1536]{5,4,3,2,1,0:T(8,128)(2,1)} %bitcast.10) | data formatting | bytes 7077888
  121.9 0.0 copy-done
  121.9 0.6 copy.12
Async XLA Ops:
  117.9 4.0 %copy-start = (f32[2,128]{1,0:T(2,128)S(1)}, f32[2,128]{1,0:T(2,128)}, u32[]{:S(2)}) copy-start(f32[2,128]{1,0:T(2,128)} %get-tuple-element.5) | copy-start | bytes 3076

commit v2 on v1

v2 whole, which is shorter than its diff:
```python
import math

import jax
import jax.numpy as jnp
from jax import lax
from jax.experimental import pallas as pl
from jax.experimental.pallas import tpu as pltpu
from jax.sharding import PartitionSpec as P

HEADS = 12
DIM = 128
TILE = 384
SPAN = 3 * TILE
EPSILON = 1e-06
SCALE = DIM**-0.5
EXP2_SCALE = SCALE * math.log2(math.e)
MESH = pl.DeviceIdType.MESH
BF16, F32 = jnp.bfloat16, jnp.float32

SWAPPED = 2
KEPT = HEADS - SWAPPED
GRAD_LAG, AHEAD, DQ_FROM, Q_FROM, RATE = 2, 3, 9, 11, 2
SLOTS = GRAD_LAG + 1
STEPS = HEADS + GRAD_LAG


def over_rows(a, b):
    return lax.dot_general(a, b, (((1,), (1,)), ((), ())), preferred_element_type=F32)


def product(a, b):
    return lax.dot_general(a, b, (((1,), (0,)), ((), ())), preferred_element_type=F32)


def inverse_norm(x):
    return lax.rsqrt(jnp.mean(x * x, axis=-1, keepdims=True) + EPSILON)


def norm_back(grad_hat, x, gain, inverse):
    projected = jnp.sum(gain * grad_hat * x, axis=-1, keepdims=True)
    return inverse * (gain * grad_hat) - x * (inverse * inverse * inverse * projected * (1.0 / DIM))


def kernel(
    seqs, dps, zs,
    q_ref, k_ref, v_ref, g_ref, gain_ref, list_ref,
    out_ref, gain_out,
    q_raw, k_raw, v_in, pair, k_hat, k_turned, exps, gprobs, low,
    stat, stat_l, stat_r, stat_ll, stat_rr, masks, gains,
    dq_own, dq_out, dq_in, results, gain_acc, first_slots, gain_slots,
    load_sem, swap_send, swap_recv, in_send, in_recv, stat_send, stat_recv, info_send, info_recv, dq_send, dq_recv,
    out_send, out_recv, keep_sem, first_send, first_recv, gain_send, gain_recv,
):
    p, s, d = lax.axis_index("pipe"), lax.axis_index("seq"), lax.axis_index("dp")

    def at(q, step):
        return (q, lax.rem(s + seqs + step, seqs), d)

    left, right = at(p, -1), at(p, 1)
    sides = (left, right)
    across = at(1 - p, 0)
    xs = seqs // zs
    x, z = s // zs, lax.rem(s, zs)
    groups = (
        (x, xs, lambda i: (p, i * zs + z, d)),
        (z, zs, lambda i: (p, x * zs + i, d)),
    )

    def columns(h):
        return pl.ds(pl.multiple_of(h * DIM, DIM), DIM)

    def remote(source, target, send, recv, device):
        return pltpu.make_async_remote_copy(
            src_ref=source, dst_ref=target, send_sem=send, recv_sem=recv,
            device_id=device, device_id_type=MESH,
        )

    def places(h):
        return (
            (q_ref, q_raw.at[h]),
            (k_ref, k_raw.at[h]),
            (g_ref, pair.at[h, 1, pl.ds(TILE, TILE)]),
            (v_ref, v_in.at[h]),
        )

    def loads(h):
        return [
            pltpu.make_async_copy(source.at[:, columns(h)], target, load_sem.at[part, h])
            for part, (source, target) in enumerate(places(h))
        ]

    def swaps(h):
        return [
            remote(
                source.at[:, columns(h)], target,
                swap_send.at[part, h - KEPT], swap_recv.at[part, h - KEPT], across,
            )
            for part, (source, target) in enumerate(places(h))
        ]

    def start_loads(h, carry):
        for copy in loads(h):
            copy.start()
        return carry

    lax.fori_loop(0, KEPT, start_loads, 0)

    barrier = pltpu.get_barrier_semaphore()
    greeted = [at(p, -1), at(p, 1), at(p, -2), at(p, 2), at(1 - p, -1), at(1 - p, 0), at(1 - p, 1)]
    for j in range(1, dps):
        greeted += [(q, s, lax.rem(d + j, dps)) for q in (p, 1 - p)]
    for mine, size, device in groups:
        greeted += [device(lax.rem(mine + j, size)) for j in range(1, size)]
    for device in greeted:
        pl.semaphore_signal(barrier, inc=1, device_id=device, device_id_type=MESH)

    def names(tile):
        named = (list_ref[0, 0] == tile) | (list_ref[0, 1] == tile) | (list_ref[0, 2] == tile)
        return jnp.where(named, 1.0, 0.0).astype(F32)

    masks[0, 1, 0:1] = jnp.full((1, TILE), jnp.where(s > 0, names(s - 1), 0.0), F32)
    masks[0, 1, 1:2] = jnp.full((1, TILE), names(s + 1), F32)
    gains[0] = gain_ref[...]

    own_masks = masks.at[0, 1]
    infos = [
        remote(own_masks, masks.at[q, t], info_send.at[e], info_recv.at[e], device)
        for e, (q, t, device) in enumerate(
            (
                (0, 2, at(p, -1)), (0, 0, at(p, 1)),
                (1, 2, at(1 - p, -1)), (1, 0, at(1 - p, 1)), (1, 1, across),
            )
        )
    ]
    infos.append(remote(gains.at[0], gains.at[1], info_send.at[5], info_recv.at[5], across))

    def send_pair(h, side):
        return remote(
            pair.at[h, :, pl.ds(TILE, TILE)], pair.at[h, :, pl.ds(2 * TILE * (1 - side), TILE)],
            in_send.at[h, side], in_recv.at[h, 1 - side], sides[side],
        )

    def send_dq(h, side):
        return remote(
            dq_out.at[h, side], dq_in.at[h, 1 - side], dq_send.at[h, side], dq_recv.at[h, 1 - side], sides[side]
        )

    def send_stats(h):
        return [
            remote(source, target.at[h], stat_send.at[h, e], stat_recv.at[h, e], device)
            for e, (source, target, device) in enumerate(
                (
                    (stat.at[h, pl.ds(0, 2)], stat_r, left),
                    (stat.at[h, pl.ds(1, 2)], stat_l, right),
                    (stat.at[h, pl.ds(0, 1)], stat_rr, at(p, -2)),
                    (stat.at[h, pl.ds(2, 1)], stat_ll, at(p, 2)),
                )
            )
        ]

    def send_result(part, h):
        return remote(
            results.at[part, h], out_ref.at[part, :, columns(h)],
            out_send.at[part, h], out_recv.at[part, h], across,
        )

    def keep_result(part, h):
        return pltpu.make_async_copy(
            results.at[part, h], out_ref.at[part, :, columns(h)], keep_sem.at[part, h - KEPT]
        )

    def give_result(part, h):
        @pl.when(h < KEPT)
        def _():
            send_result(part, h).start()

        @pl.when(h >= KEPT)
        def _():
            keep_result(part, h).start()

    def segment(h):
        return jnp.where(h >= KEPT, 1, 0)

    def normalize(h):
        @pl.when(h < KEPT)
        def _():
            for copy in loads(h):
                copy.wait()

        @pl.when(h >= KEPT)
        def _():
            for copy in swaps(h):
                copy.wait_recv()

        q = q_raw[h].astype(F32)
        pair[h, 0, TILE : 2 * TILE] = (q * inverse_norm(q) * gains[segment(h), 0:1]).astype(BF16)

    def normalize_key(h):
        k = k_raw[h].astype(F32)
        hat = k * inverse_norm(k) * gains[segment(h), 1:2]
        k_hat[h] = hat.astype(BF16)
        k_turned[h] = hat.T.astype(BF16)

    def give_pair(h):
        for side in (0, 1):
            send_pair(h, side).start()

    def scores(h):
        for side in (0, 1):
            send_pair(h, side).wait_recv()
        slot = lax.rem(h, SLOTS)
        for b in range(3):
            span = slice(b * TILE, (b + 1) * TILE)
            e = jnp.exp2(over_rows(k_hat[h], pair[h, 0, span]) * EXP2_SCALE)
            g = over_rows(v_in[h], pair[h, 1, span])
            exps[slot, :, span] = e
            gprobs[slot, :, span] = g
            stat[h, b, 0:1] = jnp.sum(e, axis=0, keepdims=True)
            stat[h, b, 1:2] = jnp.sum(e * g, axis=0, keepdims=True)
        for copy in send_stats(h):
            copy.start()

    def grads(h):
        for copy in send_stats(h):
            copy.wait_recv()
        slot, seg = lax.rem(h, SLOTS), segment(h)
        to_left = [masks[seg, t, 0:1] for t in range(3)]
        to_right = [masks[seg, t, 1:2] for t in range(3)]
        sums = (
            stat[h, 0] * to_right[0] + stat_l[h, 0] + stat_ll[h, 0] * to_left[0],
            stat[h, 1] + stat_l[h, 1] * to_left[1] + stat_r[h, 0] * to_right[1],
            stat[h, 2] * to_left[2] + stat_r[h, 1] + stat_rr[h, 0] * to_right[2],
        )
        for b in range(3):
            span = slice(b * TILE, (b + 1) * TILE)
            inverse = 1.0 / sums[b][0:1]
            delta = sums[b][1:2] * inverse
            share = (inverse * to_right[0], inverse, inverse * to_left[2])[b]
            probs = exps[slot, :, span] * share
            low[0, :, span] = probs.astype(BF16)
            low[1, :, span] = (probs * (gprobs[slot, :, span] - delta)).astype(BF16)
        results[2, h] = product(low[0], pair[h, 1]).astype(BF16)
        give_result(2, h)
        grad_hat = product(low[1], pair[h, 0]) * SCALE
        k = k_raw[h].astype(F32)
        inverse = inverse_norm(k)
        results[1, h] = norm_back(grad_hat, k, gains[seg, 1:2], inverse).astype(BF16)
        give_result(1, h)
        turned = product(k_turned[h], low[1])
        dq_out[h, 0] = turned[:, :TILE].astype(BF16)
        dq_out[h, 1] = turned[:, 2 * TILE :].astype(BF16)
        dq_own[h] = turned[:, TILE : 2 * TILE]
        gain_acc[seg, 0:1] += jnp.sum(grad_hat * k_hat[h].astype(F32), axis=0, keepdims=True) / gains[seg, 0:1]
        gain_acc[seg, 1:2] += jnp.sum(grad_hat * (k * inverse), axis=0, keepdims=True)

    def give_dq(h, carry):
        for side in (0, 1):
            send_dq(h, side).start()
        return carry

    def query_grads(h, carry):
        for side in (0, 1):
            send_dq(h, side).wait_recv()
        total = dq_own[h] + dq_in[h, 0].astype(F32) + dq_in[h, 1].astype(F32)
        q = q_raw[h].astype(F32)
        grad = norm_back((total * SCALE).T, q, gains[segment(h), 0:1], inverse_norm(q))
        results[0, h] = grad.astype(BF16)
        give_result(0, h)
        return carry

    gain_acc[...] = jnp.zeros_like(gain_acc)
    normalize(0)
    pl.semaphore_wait(barrier, len(greeted))
    give_pair(0)
    for copy in infos:
        copy.start()
    for h in range(KEPT, HEADS):
        for copy in swaps(h):
            copy.start()
    for h in range(1, AHEAD):
        normalize(h)
        give_pair(h)
    for h in range(AHEAD):
        normalize_key(h)
    for copy in infos:
        copy.wait_recv()

    def given(i):
        return jnp.clip(jnp.minimum((i - DQ_FROM + 1) * RATE, i - GRAD_LAG + 1), 0, HEADS)

    def taken(i):
        return jnp.clip(jnp.minimum((i - Q_FROM + 1) * RATE, given(i - 1)), 0, HEADS)

    def step(i, carry):
        @pl.when(i < HEADS)
        def _():
            scores(i)

        @pl.when(i + AHEAD < HEADS)
        def _():
            normalize(i + AHEAD)
            give_pair(i + AHEAD)
            normalize_key(i + AHEAD)

        @pl.when(i >= GRAD_LAG)
        def _():
            grads(i - GRAD_LAG)

        lax.fori_loop(given(i - 1), given(i), give_dq, 0)
        lax.fori_loop(taken(i - 1), taken(i), query_grads, 0)
        return carry

    lax.fori_loop(0, STEPS, step, 0)
    lax.fori_loop(given(STEPS - 1), HEADS, give_dq, 0)

    def first(j, other):
        to, sender = lax.rem(d + j, dps), lax.rem(d + dps - j, dps)
        copy = remote(
            gain_acc.at[other], first_slots.at[other, d], first_send.at[other, j], first_recv.at[other, j],
            (1 - p if other else p, s, to),
        )
        arrival = remote(
            gain_acc.at[other], first_slots.at[other, sender], first_send.at[other, j], first_recv.at[other, j],
            (1 - p if other else p, s, to),
        )
        return copy, arrival

    def later(axis, j):
        mine, size, device = groups[axis]
        to, sender = device(lax.rem(mine + j, size)), lax.rem(mine + size - j, size)
        return [
            remote(
                gain_slots.at[axis, mine], gain_slots.at[axis, slot],
                gain_send.at[axis, j - 1], gain_recv.at[axis, j - 1], to,
            )
            for slot in (mine, sender)
        ]

    rounds = [[first(j, other) for other in (0, 1) for j in range(1 - other, dps)]]
    rounds += [[later(axis, j) for j in range(1, groups[axis][1])] for axis in (0, 1)]

    def begin(r, value):
        if r == 0:
            first_slots[0, d] = value
        else:
            gain_slots[r - 1, groups[r - 1][0]] = value
        for copy, _ in rounds[r]:
            copy.start()

    def end(r):
        for _, arrival in rounds[r]:
            arrival.wait_recv()
        for copy, _ in rounds[r]:
            copy.wait_send()
        if r == 0:
            slots = [first_slots[other, j] for other in (0, 1) for j in range(dps)]
        else:
            slots = [gain_slots[r - 1, j] for j in range(groups[r - 1][1])]
        total = slots[0]
        for slot in slots[1:]:
            total = total + slot
        return total

    begin(0, gain_acc[0])
    done, rest = taken(STEPS - 1), HEADS - taken(STEPS - 1)
    marks = [done, done + rest // 2, done + rest * 3 // 4, HEADS]
    for r in range(3):
        lax.fori_loop(marks[r], marks[r + 1], query_grads, 0)
        total = end(r)
        if r < 2:
            begin(r + 1, total)
        else:
            gain_out[...] = total * (1.0 / math.sqrt(dps * seqs * TILE * HEADS))

    for copy in infos:
        copy.wait_send()

    def finish(h, carry):
        for side in (0, 1):
            send_pair(h, side).wait_send()
            send_dq(h, side).wait_send()
        for copy in send_stats(h):
            copy.wait_send()

        @pl.when(h < KEPT)
        def _():
            for part in range(3):
                send_result(part, h).wait()

        @pl.when(h >= KEPT)
        def _():
            for copy in swaps(h):
                copy.wait_send()
            for part in range(3):
                keep_result(part, h).wait()

        return carry

    lax.fori_loop(0, HEADS, finish, 0)


def solution(mesh):
    seqs, dps = mesh.shape["seq"], mesh.shape["dp"]
    zs = 4
    dma, vmem = pltpu.SemaphoreType.DMA, pltpu.VMEM

    def body(*refs):
        kernel(seqs, dps, zs, *refs)

    call = pl.pallas_call(
        body,
        out_shape=(
            pltpu.VMEM((3, TILE, HEADS * DIM), BF16),
            jax.ShapeDtypeStruct((2, DIM), F32),
        ),
        in_specs=[pl.BlockSpec(memory_space=pl.ANY)] * 4
        + [pl.BlockSpec(memory_space=pltpu.VMEM), pl.BlockSpec(memory_space=pltpu.SMEM)],
        out_specs=(pl.BlockSpec(memory_space=pltpu.VMEM), pl.BlockSpec(memory_space=pltpu.VMEM)),
        scratch_shapes=[
            vmem((HEADS, TILE, DIM), BF16),
            vmem((HEADS, TILE, DIM), BF16),
            vmem((HEADS, TILE, DIM), BF16),
            vmem((HEADS, 2, SPAN, DIM), BF16),
            vmem((HEADS, TILE, DIM), BF16),
            vmem((HEADS, DIM, TILE), BF16),
            vmem((SLOTS, TILE, SPAN), F32),
            vmem((SLOTS, TILE, SPAN), F32),
            vmem((2, TILE, SPAN), BF16),
            vmem((HEADS, 3, 2, TILE), F32),
            vmem((HEADS, 2, 2, TILE), F32),
            vmem((HEADS, 2, 2, TILE), F32),
            vmem((HEADS, 1, 2, TILE), F32),
            vmem((HEADS, 1, 2, TILE), F32),
            vmem((2, 3, 2, TILE), F32),
            vmem((2, 2, DIM), F32),
            vmem((HEADS, DIM, TILE), F32),
            vmem((HEADS, 2, DIM, TILE), BF16),
            vmem((HEADS, 2, DIM, TILE), BF16),
            vmem((3, HEADS, TILE, DIM), BF16),
            vmem((2, 2, DIM), F32),
            vmem((2, dps, 2, DIM), F32),
            vmem((2, 4, 2, DIM), F32),
            dma((4, HEADS)),
            dma((4, SWAPPED)),
            dma((4, SWAPPED)),
            dma((HEADS, 2)),
            dma((HEADS, 2)),
            dma((HEADS, 4)),
            dma((HEADS, 4)),
            dma((6,)),
            dma((6,)),
            dma((HEADS, 2)),
            dma((HEADS, 2)),
            dma((3, HEADS)),
            dma((3, HEADS)),
            dma((3, SWAPPED)),
            dma((2, dps)),
            dma((2, dps)),
            dma((2, 3)),
            dma((2, 3)),
        ],
        compiler_params=pltpu.CompilerParams(
            collective_id=0, has_side_effects=True, vmem_limit_bytes=58 * 2**20
        ),
        cost_estimate=pl.CostEstimate(
            flops=10 * TILE * SPAN * HEADS * DIM,
            bytes_accessed=7 * 2 * TILE * HEADS * DIM,
            transcendentals=TILE * SPAN * HEADS,
        ),
    )

    def local(queries, keys, values, grad_out, norm_gains, kv_tiles):
        grads, gain_grads = call(
            queries[0, 0, 0], keys[0, 0, 0], values[0, 0, 0], grad_out[0, 0, 0],
            norm_gains[0], kv_tiles[0, 0],
        )
        return grads[None, :, None, None], gain_grads[None]

    tokens = P("pipe", "dp", "seq", None, None)
    return jax.shard_map(
        local,
        mesh=mesh,
        in_specs=(tokens,) * 4 + (P("pipe", None, None), P("pipe", "dp", "seq", None)),
        out_specs=(P("pipe", None, "dp", "seq", None, None), P("pipe", None, None)),
        check_vma=False,
    )
```

time: 123 us -> 102 us (0.83)
  Pallas kernels: 117 us -> 98.6 us
  local copies, waits for them, and re-layouts: 4.59 us -> 2.36 us
    pallas_call x1, Pallas kernels: 117 us -> 98.6 us  [local(): call(queries[0, 0, 0], keys[0, 0, 0], values[0, 0, 0], grad_out[0, 0, 0],...]
    unnamed x4, local copies, waits for them, and re-layouts: 4.59 us -> 2.36 us
where the time goes in v2:
time: 102 us
  Pallas kernels  98.6 us (97%)
  local copies, waits for them, and re-layouts  2.36 us (2%)
    pallas_call x1, Pallas kernels, local(): call(queries[0, 0, 0], keys[0, 0, 0], values[0, 0, 0], grad_out[0, 0, 0],...  98.6 us
    unnamed x4, local copies, waits for them, and re-layouts  2.36 us

profile of v2, /device:TPU:0, one launch (start us, length us, event | category | flops | bytes accessed | tf_op | source)
XLA Modules:
  0.0 101.7 jit_solution(14388867339221585130)
XLA Ops:
  0.6 98.6 %shard_map.77 = (bf16[3,384,1536]{2,1,0:T(8,128)(2,1)S(1)}, f32[2,128]{1,0:T(2,128)}) custom-call(bf16[384,1536]{1,0:T(8,128)(2,1)} %bitcast.12, bf16[384,1536]{1,0:T(8,128)(2,1)} %bitcast.13, bf16[384,1536]{1,0:T(8,128)(2,1)} %bitcast.14, bf16[384,1536]{1,0:T(8,128)(2,1)} %bitcast.15, f32[2,128]{1,0:T(2,128)} %bitcast.16, s32[1,3]{1,0:T(1,128)} %bitcast.17), custom_call_target="tpu_custom_call" | custom-call | flops 6794772480 | bytes 8257536 | tf_op jit(solution)/shard_map/pallas_call | solution.py:473
  99.3 0.0 copy-start
  99.3 1.8 %copy.11 = bf16[1,3,1,1,384,1536]{5,4,3,2,1,0:T(8,128)(2,1)} copy(bf16[1,3,1,1,384,1536]{5,4,3,2,1,0:T(8,128)(2,1)S(1)} %bitcast.10) | data formatting | bytes 7077888
  101.1 0.0 copy-done
  101.1 0.6 copy.12
Async XLA Ops:
  99.3 1.8 %copy-start = (f32[2,128]{1,0:T(2,128)S(1)}, f32[2,128]{1,0:T(2,128)}, u32[]{:S(2)}) copy-start(f32[2,128]{1,0:T(2,128)} %get-tuple-element.5) | copy-start | bytes 3076

commit v3 on v2

--- a/solution.py
+++ b/solution.py
@@ -17,9 +17,9 @@
 MESH = pl.DeviceIdType.MESH
 BF16, F32 = jnp.bfloat16, jnp.float32
 
-SWAPPED = 2
+SWAPPED = 3
 KEPT = HEADS - SWAPPED
-GRAD_LAG, AHEAD, DQ_FROM, Q_FROM, RATE = 2, 3, 9, 11, 2
+GRAD_LAG, AHEAD, DQ_FROM, RATE, EARLY, WAIT = 2, 3, 9, 2, 0, 3
 SLOTS = GRAD_LAG + 1
 STEPS = HEADS + GRAD_LAG
 
@@ -49,7 +49,7 @@
     stat, stat_l, stat_r, stat_ll, stat_rr, masks, gains,
     dq_own, dq_out, dq_in, results, gain_acc, first_slots, gain_slots,
     load_sem, swap_send, swap_recv, in_send, in_recv, stat_send, stat_recv, info_send, info_recv, dq_send, dq_recv,
-    out_send, out_recv, keep_sem, first_send, first_recv, gain_send, gain_recv,
+    out_send, out_recv, first_send, first_recv, gain_send, gain_recv,
 ):
     p, s, d = lax.axis_index("pipe"), lax.axis_index("seq"), lax.axis_index("dp")
 
@@ -93,7 +93,7 @@
         return [
             remote(
                 source.at[:, columns(h)], target,
-                swap_send.at[part, h - KEPT], swap_recv.at[part, h - KEPT], across,
+                swap_send.at[part], swap_recv.at[part, h - KEPT], across,
             )
             for part, (source, target) in enumerate(places(h))
         ]
@@ -137,17 +137,17 @@
     def send_pair(h, side):
         return remote(
             pair.at[h, :, pl.ds(TILE, TILE)], pair.at[h, :, pl.ds(2 * TILE * (1 - side), TILE)],
-            in_send.at[h, side], in_recv.at[h, 1 - side], sides[side],
+            in_send.at[side], in_recv.at[h, 1 - side], sides[side],
         )
 
     def send_dq(h, side):
         return remote(
-            dq_out.at[h, side], dq_in.at[h, 1 - side], dq_send.at[h, side], dq_recv.at[h, 1 - side], sides[side]
+            dq_out.at[h, side], dq_in.at[h, 1 - side], dq_send.at[side], dq_recv.at[h, 1 - side], sides[side]
         )
 
     def send_stats(h):
         return [
-            remote(source, target.at[h], stat_send.at[h, e], stat_recv.at[h, e], device)
+            remote(source, target.at[h], stat_send.at[e], stat_recv.at[h, e], device)
             for e, (source, target, device) in enumerate(
                 (
                     (stat.at[h, pl.ds(0, 2)], stat_r, left),
@@ -161,22 +161,18 @@
     def send_result(part, h):
         return remote(
             results.at[part, h], out_ref.at[part, :, columns(h)],
-            out_send.at[part, h], out_recv.at[part, h], across,
-        )
-
-    def keep_result(part, h):
-        return pltpu.make_async_copy(
-            results.at[part, h], out_ref.at[part, :, columns(h)], keep_sem.at[part, h - KEPT]
-        )
-
-    def give_result(part, h):
+            out_send.at[0], out_recv.at[0], across,
+        )
+
+    def give_result(part, h, value):
         @pl.when(h < KEPT)
         def _():
+            results[part, h] = value
             send_result(part, h).start()
 
         @pl.when(h >= KEPT)
         def _():
-            keep_result(part, h).start()
+            out_ref[part, :, columns(h)] = value
 
     def segment(h):
         return jnp.where(h >= KEPT, 1, 0)
@@ -239,13 +235,11 @@
             probs = exps[slot, :, span] * share
             low[0, :, span] = probs.astype(BF16)
             low[1, :, span] = (probs * (gprobs[slot, :, span] - delta)).astype(BF16)
-        results[2, h] = product(low[0], pair[h, 1]).astype(BF16)
-        give_result(2, h)
+        give_result(2, h, product(low[0], pair[h, 1]).astype(BF16))
         grad_hat = product(low[1], pair[h, 0]) * SCALE
         k = k_raw[h].astype(F32)
         inverse = inverse_norm(k)
-        results[1, h] = norm_back(grad_hat, k, gains[seg, 1:2], inverse).astype(BF16)
-        give_result(1, h)
+        give_result(1, h, norm_back(grad_hat, k, gains[seg, 1:2], inverse).astype(BF16))
         turned = product(k_turned[h], low[1])
         dq_out[h, 0] = turned[:, :TILE].astype(BF16)
         dq_out[h, 1] = turned[:, 2 * TILE :].astype(BF16)
@@ -264,8 +258,7 @@
         total = dq_own[h] + dq_in[h, 0].astype(F32) + dq_in[h, 1].astype(F32)
         q = q_raw[h].astype(F32)
         grad = norm_back((total * SCALE).T, q, gains[segment(h), 0:1], inverse_norm(q))
-        results[0, h] = grad.astype(BF16)
-        give_result(0, h)
+        give_result(0, h, grad.astype(BF16))
         return carry
 
     gain_acc[...] = jnp.zeros_like(gain_acc)
@@ -282,14 +275,14 @@
         give_pair(h)
     for h in range(AHEAD):
         normalize_key(h)
-    for copy in infos:
-        copy.wait_recv()
 
     def given(i):
-        return jnp.clip(jnp.minimum((i - DQ_FROM + 1) * RATE, i - GRAD_LAG + 1), 0, HEADS)
+        early = (jnp.clip(i - GRAD_LAG, 0, HEADS) * EARLY) // 6
+        late = (i - DQ_FROM + 1) * RATE
+        return jnp.clip(jnp.minimum(jnp.maximum(early, late), i - GRAD_LAG + 1), 0, HEADS)
 
     def taken(i):
-        return jnp.clip(jnp.minimum((i - Q_FROM + 1) * RATE, given(i - 1)), 0, HEADS)
+        return given(i - WAIT)
 
     def step(i, carry):
         @pl.when(i < HEADS)
@@ -301,6 +294,11 @@
             normalize(i + AHEAD)
             give_pair(i + AHEAD)
             normalize_key(i + AHEAD)
+
+        @pl.when(i == 0)
+        def _():
+            for copy in infos:
+                copy.wait_recv()
 
         @pl.when(i >= GRAD_LAG)
         def _():
@@ -375,28 +373,22 @@
     for copy in infos:
         copy.wait_send()
 
-    def finish(h, carry):
-        for side in (0, 1):
-            send_pair(h, side).wait_send()
-            send_dq(h, side).wait_send()
-        for copy in send_stats(h):
-            copy.wait_send()
-
-        @pl.when(h < KEPT)
-        def _():
-            for part in range(3):
-                send_result(part, h).wait()
-
-        @pl.when(h >= KEPT)
-        def _():
-            for copy in swaps(h):
-                copy.wait_send()
-            for part in range(3):
-                keep_result(part, h).wait()
-
-        return carry
-
-    lax.fori_loop(0, HEADS, finish, 0)
+    kept, swapped = pl.ds(0, KEPT * DIM), pl.ds(KEPT * DIM, SWAPPED * DIM)
+    for side in (0, 1):
+        own = pair.at[:, :, pl.ds(TILE, TILE)]
+        remote(own, own, in_send.at[side], in_send.at[side], sides[side]).wait_send()
+        own = dq_out.at[:, side]
+        remote(own, own, dq_send.at[side], dq_send.at[side], sides[side]).wait_send()
+    for e, own in enumerate(
+        (stat.at[:, pl.ds(0, 2)], stat.at[:, pl.ds(1, 2)], stat.at[:, pl.ds(0, 1)], stat.at[:, pl.ds(2, 1)])
+    ):
+        remote(own, own, stat_send.at[e], stat_send.at[e], left).wait_send()
+    for part, source in enumerate((q_ref, k_ref, g_ref, v_ref)):
+        own = source.at[:, swapped]
+        remote(own, own, swap_send.at[part], swap_send.at[part], across).wait_send()
+    final = remote(results, out_ref.at[:, :, kept], out_send.at[0], out_recv.at[0], across)
+    final.wait_send()
+    final.wait_recv()
 
 
 def solution(mesh):
@@ -436,24 +428,23 @@
             vmem((HEADS, DIM, TILE), F32),
             vmem((HEADS, 2, DIM, TILE), BF16),
             vmem((HEADS, 2, DIM, TILE), BF16),
-            vmem((3, HEADS, TILE, DIM), BF16),
+            vmem((3, KEPT, TILE, DIM), BF16),
             vmem((2, 2, DIM), F32),
             vmem((2, dps, 2, DIM), F32),
             vmem((2, 4, 2, DIM), F32),
             dma((4, HEADS)),
+            dma((4,)),
             dma((4, SWAPPED)),
-            dma((4, SWAPPED)),
+            dma((2,)),
             dma((HEADS, 2)),
-            dma((HEADS, 2)),
-            dma((HEADS, 4)),
+            dma((4,)),
             dma((HEADS, 4)),
             dma((6,)),
             dma((6,)),
+            dma((2,)),
             dma((HEADS, 2)),
-            dma((HEADS, 2)),
-            dma((3, HEADS)),
-            dma((3, HEADS)),
-            dma((3, SWAPPED)),
+            dma((1,)),
+            dma((1,)),
             dma((2, dps)),
             dma((2, dps)),
             dma((2, 3)),

time: 102 us -> 99.2 us (0.973)
  Pallas kernels: 98.6 us -> 96 us
    pallas_call x1, Pallas kernels: 98.6 us -> 96 us  [local(): call(queries[0, 0, 0], keys[0, 0, 0], values[0, 0, 0], grad_out[0, 0, 0],...]
where the time goes in v3:
time: 99.2 us; the launch traced here: 99 us
  Pallas kernels  96 us (97%)
  local copies, waits for them, and re-layouts  2.36 us (2%)
    pallas_call x1, Pallas kernels, local(): call(queries[0, 0, 0], keys[0, 0, 0], values[0, 0, 0], grad_out[0, 0, 0],...  96 us
    unnamed x4, local copies, waits for them, and re-layouts  2.36 us

profile of v3, /device:TPU:0, one launch (start us, length us, event | category | flops | bytes accessed | tf_op | source)
XLA Modules:
  0.0 99.0 jit_solution(6305612440732078468)
XLA Ops:
  0.6 96.0 %shard_map.77 = (bf16[3,384,1536]{2,1,0:T(8,128)(2,1)S(1)}, f32[2,128]{1,0:T(2,128)}) custom-call(bf16[384,1536]{1,0:T(8,128)(2,1)} %bitcast.12, bf16[384,1536]{1,0:T(8,128)(2,1)} %bitcast.13, bf16[384,1536]{1,0:T(8,128)(2,1)} %bitcast.14, bf16[384,1536]{1,0:T(8,128)(2,1)} %bitcast.15, f32[2,128]{1,0:T(2,128)} %bitcast.16, s32[1,3]{1,0:T(1,128)} %bitcast.17), custom_call_target="tpu_custom_call" | custom-call | flops 6794772480 | bytes 8257536 | tf_op jit(solution)/shard_map/pallas_call | solution.py:464
  96.7 0.0 copy-start
  96.7 1.8 %copy.11 = bf16[1,3,1,1,384,1536]{5,4,3,2,1,0:T(8,128)(2,1)} copy(bf16[1,3,1,1,384,1536]{5,4,3,2,1,0:T(8,128)(2,1)S(1)} %bitcast.10) | data formatting | bytes 7077888
  98.5 0.0 copy-done
  98.5 0.6 copy.12
Async XLA Ops:
  96.7 1.8 %copy-start = (f32[2,128]{1,0:T(2,128)S(1)}, f32[2,128]{1,0:T(2,128)}, u32[]{:S(2)}) copy-start(f32[2,128]{1,0:T(2,128)} %get-tuple-element.5) | copy-start | bytes 3076

commit v4 on v3

--- a/solution.py
+++ b/solution.py
@@ -103,8 +103,6 @@
             copy.start()
         return carry
 
-    lax.fori_loop(0, KEPT, start_loads, 0)
-
     barrier = pltpu.get_barrier_semaphore()
     greeted = [at(p, -1), at(p, 1), at(p, -2), at(p, 2), at(1 - p, -1), at(1 - p, 0), at(1 - p, 1)]
     for j in range(1, dps):
@@ -113,6 +111,7 @@
         greeted += [device(lax.rem(mine + j, size)) for j in range(1, size)]
     for device in greeted:
         pl.semaphore_signal(barrier, inc=1, device_id=device, device_id_type=MESH)
+    start_loads(0, 0)
 
     def names(tile):
         named = (list_ref[0, 0] == tile) | (list_ref[0, 1] == tile) | (list_ref[0, 2] == tile)
@@ -267,7 +266,10 @@
     give_pair(0)
     for copy in infos:
         copy.start()
-    for h in range(KEPT, HEADS):
+    for copy in swaps(KEPT):
+        copy.start()
+    lax.fori_loop(1, KEPT, start_loads, 0)
+    for h in range(KEPT + 1, HEADS):
         for copy in swaps(h):
             copy.start()
     for h in range(1, AHEAD):

time: 99.2 us -> 99.1 us (level)
  no operation moved by 1% of the time
where the time goes in v4:
time: 99.1 us; the launch traced here: 98.9 us
  Pallas kernels  95.9 us (97%)
  local copies, waits for them, and re-layouts  2.36 us (2%)
    pallas_call x1, Pallas kernels, local(): call(queries[0, 0, 0], keys[0, 0, 0], values[0, 0, 0], grad_out[0, 0, 0],...  95.9 us
    unnamed x4, local copies, waits for them, and re-layouts  2.36 us

profile of v4, /device:TPU:0, one launch (start us, length us, event | category | flops | bytes accessed | tf_op | source)
XLA Modules:
  0.0 98.9 jit_solution(10475321579630100118)
XLA Ops:
  0.6 95.9 %shard_map.77 = (bf16[3,384,1536]{2,1,0:T(8,128)(2,1)S(1)}, f32[2,128]{1,0:T(2,128)}) custom-call(bf16[384,1536]{1,0:T(8,128)(2,1)} %bitcast.12, bf16[384,1536]{1,0:T(8,128)(2,1)} %bitcast.13, bf16[384,1536]{1,0:T(8,128)(2,1)} %bitcast.14, bf16[384,1536]{1,0:T(8,128)(2,1)} %bitcast.15, f32[2,128]{1,0:T(2,128)} %bitcast.16, s32[1,3]{1,0:T(1,128)} %bitcast.17), custom_call_target="tpu_custom_call" | custom-call | flops 6794772480 | bytes 8257536 | tf_op jit(solution)/shard_map/pallas_call | solution.py:466
  96.5 0.0 copy-start
  96.5 1.8 %copy.11 = bf16[1,3,1,1,384,1536]{5,4,3,2,1,0:T(8,128)(2,1)} copy(bf16[1,3,1,1,384,1536]{5,4,3,2,1,0:T(8,128)(2,1)S(1)} %bitcast.10) | data formatting | bytes 7077888
  98.3 0.0 copy-done
  98.3 0.6 copy.12
Async XLA Ops:
  96.5 1.8 %copy-start = (f32[2,128]{1,0:T(2,128)S(1)}, f32[2,128]{1,0:T(2,128)}, u32[]{:S(2)}) copy-start(f32[2,128]{1,0:T(2,128)} %get-tuple-element.5) | copy-start | bytes 3076

commit v5 on v3

--- a/solution.py
+++ b/solution.py
@@ -19,7 +19,7 @@
 
 SWAPPED = 3
 KEPT = HEADS - SWAPPED
-GRAD_LAG, AHEAD, DQ_FROM, RATE, EARLY, WAIT = 2, 3, 9, 2, 0, 3
+GRAD_LAG, AHEAD, DQ_FROM, RATE, EARLY, WAIT = 2, 3, 9, 2, 1, 3
 SLOTS = GRAD_LAG + 1
 STEPS = HEADS + GRAD_LAG
 

time: 99.2 us -> 99.2 us (level)
  no operation moved by 1% of the time
where the time goes in v5:
time: 99.2 us; the launch traced here: 99 us
  Pallas kernels  96 us (97%)
  local copies, waits for them, and re-layouts  2.36 us (2%)
    pallas_call x1, Pallas kernels, local(): call(queries[0, 0, 0], keys[0, 0, 0], values[0, 0, 0], grad_out[0, 0, 0],...  96 us
    unnamed x4, local copies, waits for them, and re-layouts  2.36 us

profile of v5, /device:TPU:0, one launch (start us, length us, event | category | flops | bytes accessed | tf_op | source)
XLA Modules:
  0.0 99.0 jit_solution(12332921424111544261)
XLA Ops:
  0.6 96.0 %shard_map.77 = (bf16[3,384,1536]{2,1,0:T(8,128)(2,1)S(1)}, f32[2,128]{1,0:T(2,128)}) custom-call(bf16[384,1536]{1,0:T(8,128)(2,1)} %bitcast.12, bf16[384,1536]{1,0:T(8,128)(2,1)} %bitcast.13, bf16[384,1536]{1,0:T(8,128)(2,1)} %bitcast.14, bf16[384,1536]{1,0:T(8,128)(2,1)} %bitcast.15, f32[2,128]{1,0:T(2,128)} %bitcast.16, s32[1,3]{1,0:T(1,128)} %bitcast.17), custom_call_target="tpu_custom_call" | custom-call | flops 6794772480 | bytes 8257536 | tf_op jit(solution)/shard_map/pallas_call | solution.py:464
  96.7 0.0 copy-start
  96.7 1.8 %copy.11 = bf16[1,3,1,1,384,1536]{5,4,3,2,1,0:T(8,128)(2,1)} copy(bf16[1,3,1,1,384,1536]{5,4,3,2,1,0:T(8,128)(2,1)S(1)} %bitcast.10) | data formatting | bytes 7077888
  98.5 0.0 copy-done
  98.5 0.6 copy.12
Async XLA Ops:
  96.7 1.8 %copy-start = (f32[2,128]{1,0:T(2,128)S(1)}, f32[2,128]{1,0:T(2,128)}, u32[]{:S(2)}) copy-start(f32[2,128]{1,0:T(2,128)} %get-tuple-element.5) | copy-start | bytes 3076
